TPU v7x, 128 devices: a whole 4x4x4 slice. The times are simulated.
128 devices in a mesh: ma: 8 (over y, x_hi), blk: 16 (over x_lo, z, core).
Axes of the slice: x: 4 (x_hi: 2, x_lo: 2; x = x_hi * 2 + x_lo), y: 4, z: 4, core: 2. Of those that a mesh axis runs over, the one named last changes fastest.
Arguments:
- cycle_rows: float32 [65536, 2048], P(('ma', 'blk')), may hold values from -6 to 6
- owner_map: int32 [16], replicated, may hold values from 0 to 15, each once
- factors: float32 [4, 16, 1024, 64, 128], P(None, 'ma', 'blk'), may hold values from -0.5 to 0.5
Outputs:
- coeffs: float32 [16, 1024, 64, 128], P('ma', 'blk')
Inputs may be any that keep to these rules, and one draw needn't show every extreme that they name: owner_map is a permutation of the m-blocks; slot q of factors and of coeffs belongs to m-block owner_map[q].
All inputs are finite; a program needn't handle non-finite values.
Results may differ from a plain program's by a relative error of at most 0.0001.
Values sent between devices are 32-bit elements; how exact they have to be, the bound alone decides.
No kernel may reach another device: no remote copies, remote signals or barrier semaphores. Data moves between devices by JAX's collectives and lax.ppermute only.
A program may use at most 128 MiB of HBM per device.

v0:
```python
import jax
import jax.numpy as jnp
from jax import lax
from jax.sharding import PartitionSpec as P


def partner(x, axis, bit):
    return lax.ppermute(x, axis, [(i, i ^ 1 << bit) for i in range(lax.axis_size(axis))])


def level_product(factor_now, own_state, partner_state):
    dims = (((3,), (2,)), ((0, 1), (0, 1)))
    stacked = jnp.concatenate([own_state, partner_state], axis=2)
    return lax.dot_general(
        factor_now,
        stacked,
        dims,
        precision=lax.Precision.HIGHEST,
        preferred_element_type=jnp.float32,
    )


def slot_order(rows, owner_map, block_cols):
    cycle_count = rows.shape[0]
    block_count = owner_map.shape[0]
    blocks = jnp.transpose(rows.reshape(cycle_count, block_count, block_cols), (1, 0, 2))
    return jnp.take(blocks, owner_map, axis=0)


def on_device(cycle_rows, owner_map, factors):
    block_count = owner_map.shape[0]
    block_cols = cycle_rows.shape[1] // block_count
    level_count = factors.shape[0]
    local_blocks = factors.shape[1]
    group_count = factors.shape[2]
    rank_size = factors.shape[3]
    state_shape = (local_blocks, group_count, rank_size, block_cols)
    bit_count = lax.axis_size("blk").bit_length() - 1
    ordered = slot_order(cycle_rows, owner_map, block_cols)
    grouped = lax.all_to_all(ordered, "ma", split_axis=0, concat_axis=1, tiled=True)
    coeff_state = grouped.reshape(state_shape)
    first_state = partner(coeff_state, "blk", 0)
    coeff_state = level_product(factors[0], coeff_state, first_state)
    for level_index in range(1, level_count):
        partner_state = partner(coeff_state, "blk", level_index % bit_count)
        coeff_state = level_product(factors[level_index], coeff_state, partner_state)
    return coeff_state


def solution(mesh):
    placed = (P(("ma", "blk"), None), P(), P(None, "ma", "blk", None, None))
    return jax.shard_map(
        on_device, mesh=mesh, in_specs=placed, out_specs=P("ma", "blk", None, None), check_vma=False
    )
```

profile of v0, /device:TPU:0, one launch (start us, length us, event | category | flops | bytes accessed | tf_op | source)
XLA Modules:
  0.0 401.1 jit_solution(1815906856932999543)
XLA Ops:
  0.0 0.7 compare_and_fusion
  0.7 0.7 compare_select_fusion
  1.3 5.3 %copy.5 = f32[512,2048]{0,1:T(8,128)} copy(f32[512,2048]{1,0:T(8,128)} %param.3) | data formatting | bytes 8388608 | tf_op args[0]
  6.7 5.3 %copy.6 = f32[512,16,128]{2,0,1:T(8,128)} copy(f32[512,16,128]{0,2,1:T(8,128)} %bitcast.36) | data formatting | bytes 8388608 | tf_op jit(solution)/shard_map/reshape | solution.py:26
  12.0 5.0 %gather_fusion = f32[16,512,128]{2,1,0:T(8,128)} fusion(f32[16,512,128]{2,1,0:T(8,128)} %bitcast.34, s32[1024]{0:T(1024)S(1)} %pad_clamp_fusion), kind=kCustom, calls=%fused_computation | custom fusion | bytes 8388672 | tf_op jit(solution)/shard_map/jit(_take)/gather | solution.py:27
  17.0 2.6 broadcast_select_fusion
  19.7 0.0 slice-start
  19.7 58.0 %all_to_all.15 = f32[16,512,128]{2,1,0:T(8,128)S(1)} all-to-all(f32[16,512,128]{2,1,0:T(8,128)S(1)} %broadcast_select_fusion), channel_id=1, replica_groups=mesh['ma'=8,'blk'=16] {'ma'}, dimensions={0} | all-to-all | bytes 8388608 | tf_op jit(solution)/shard_map/all_to_all | solution.py:40
  77.7 0.0 slice-start.1
  77.7 0.4 copy.7
  78.0 0.0 slice-start.2
  78.1 0.0 slice-start.3
  78.1 0.1 collective-permute-start
  78.2 7.3 %collective-permute-done = f32[2,64,64,128]{3,2,1,0:T(8,128)} collective-permute-done((f32[2,64,64,128]{3,2,1,0:T(8,128)S(1)}, f32[2,64,64,128]{3,2,1,0:T(8,128)}, u32[]{:S(2)}, u32[]{:S(2)}) %collective-permute-start) | collective-permute-done | bytes 4194336 | tf_op jit(solution)/shard_map/ppermute | solution.py:8
  85.4 9.8 %fusion.39 = f32[2,64,64,128]{3,2,1,0:T(8,128)S(1)} fusion(f32[4,2,64,64,128]{4,3,2,1,0:T(8,128)} %param.5, f32[2,64,64,128]{3,2,1,0:T(8,128)} %collective-permute-done, f32[2,64,64,128]{3,2,1,0:T(8,128)S(1)} %bitcast.38), kind=kOutput, calls=%fused_computation.28 | convolution fusion | flops 1612709888 | bytes 16777216 | tf_op jit(solution)/shard_map/dot_general | solution.py:14
  95.2 2.0 collective-permute-start.1
  97.2 91.0 %collective-permute-done.1 = f32[2,64,64,128]{3,2,1,0:T(8,128)} collective-permute-done((f32[2,64,64,128]{3,2,1,0:T(8,128)S(1)}, f32[2,64,64,128]{3,2,1,0:T(8,128)}, u32[]{:S(2)}, u32[]{:S(2)}) %collective-permute-start.1) | collective-permute-done | bytes 4194336 | tf_op jit(solution)/shard_map/ppermute | solution.py:8
  188.2 0.0 slice-done
  188.2 0.0 slice-done.1
  188.2 0.0 slice-done.2
  188.2 0.0 slice-done.3
  188.2 9.3 %fusion.34 = f32[2,64,64,128]{3,2,1,0:T(8,128)S(1)} fusion(f32[4,2,64,64,128]{4,3,2,1,0:T(8,128)S(1)} %bitcast.40, f32[2,64,64,128]{3,2,1,0:T(8,128)} %collective-permute-done.1, f32[2,64,64,128]{3,2,1,0:T(8,128)S(1)} %fusion.39), kind=kOutput, calls=%fused_computation.27 | convolution fusion | flops 1612709888 | bytes 16777216 | tf_op jit(solution)/shard_map/dot_general | solution.py:14
  197.5 4.0 collective-permute-start.2
  201.5 90.1 %collective-permute-done.2 = f32[2,64,64,128]{3,2,1,0:T(8,128)} collective-permute-done((f32[2,64,64,128]{3,2,1,0:T(8,128)S(1)}, f32[2,64,64,128]{3,2,1,0:T(8,128)}, u32[]{:S(2)}, u32[]{:S(2)}) %collective-permute-start.2) | collective-permute-done | bytes 4194336 | tf_op jit(solution)/shard_map/ppermute | solution.py:8
  291.6 9.3 %fusion.29 = f32[2,64,64,128]{3,2,1,0:T(8,128)S(1)} fusion(f32[4,2,64,64,128]{4,3,2,1,0:T(8,128)S(1)} %bitcast.40, f32[2,64,64,128]{3,2,1,0:T(8,128)} %collective-permute-done.2, f32[2,64,64,128]{3,2,1,0:T(8,128)S(1)} %fusion.34), kind=kOutput, calls=%fused_computation.26 | convolution fusion | flops 1612709888 | bytes 16777216 | tf_op jit(solution)/shard_map/dot_general | solution.py:14
  301.0 1.3 collective-permute-start.3
  302.2 89.9 %collective-permute-done.3 = f32[2,64,64,128]{3,2,1,0:T(8,128)S(1)} collective-permute-done((f32[2,64,64,128]{3,2,1,0:T(8,128)S(1)}, f32[2,64,64,128]{3,2,1,0:T(8,128)S(1)}, u32[]{:S(2)}, u32[]{:S(2)}) %collective-permute-start.3) | collective-permute-done | bytes 4194336 | tf_op jit(solution)/shard_map/ppermute | solution.py:8
  392.2 8.9 %fusion.24 = f32[2,64,64,128]{3,2,1,0:T(8,128)} fusion(f32[4,2,64,64,128]{4,3,2,1,0:T(8,128)S(1)} %bitcast.40, f32[2,64,64,128]{3,2,1,0:T(8,128)S(1)} %collective-permute-done.3, f32[2,64,64,128]{3,2,1,0:T(8,128)S(1)} %fusion.29), kind=kOutput, calls=%fused_computation.25 | convolution fusion | flops 1612709888 | bytes 16777216 | tf_op jit(solution)/shard_map/dot_general | solution.py:14
  (2 shorter events, 0.0 us)
Async XLA Ops:
  19.7 168.5 %slice-start = ((s8[16777216]{0:T(1024)(128)(4,1)}), s8[4194304]{0:T(1024)(128)(4,1)S(1)}, s32[]{:S(2)}) async-start(s8[16777216]{0:T(1024)(128)(4,1)} %bitcast.39), calls=%async_computation.1 | async-start | bytes 8388608
  77.7 110.5 %slice-start.1 = ((s8[16777216]{0:T(1024)(128)(4,1)}), s8[4194304]{0:T(1024)(128)(4,1)S(1)}, s32[]{:S(2)}) async-start(s8[16777216]{0:T(1024)(128)(4,1)} %bitcast.39), calls=%async_computation.2 | async-start | bytes 8388608
  78.0 110.2 %slice-start.2 = ((s8[16777216]{0:T(1024)(128)(4,1)}), s8[4194304]{0:T(1024)(128)(4,1)S(1)}, s32[]{:S(2)}) async-start(s8[16777216]{0:T(1024)(128)(4,1)} %bitcast.39), calls=%async_computation.3 | async-start | bytes 8388608
  78.1 110.1 %slice-start.3 = ((s8[16777216]{0:T(1024)(128)(4,1)}), s8[4194304]{0:T(1024)(128)(4,1)S(1)}, s32[]{:S(2)}) async-start(s8[16777216]{0:T(1024)(128)(4,1)} %bitcast.39), calls=%async_computation.4 | async-start | bytes 8388608
  78.1 7.4 %collective-permute-start = (f32[2,64,64,128]{3,2,1,0:T(8,128)S(1)}, f32[2,64,64,128]{3,2,1,0:T(8,128)}, u32[]{:S(2)}, u32[]{:S(2)}) collective-permute-start(f32[2,64,64,128]{3,2,1,0:T(8,128)S(1)} %bitcast.37), channel_id=1, source_target_pairs={{0,1},{1,0},{2,3},{3,2},{4,5},{5,4},{6,7},{7,6},{8,9},{9,8},{10,11... | collective-permute-start | bytes 12582920 | tf_op jit(solution)/shard_map/ppermute | solution.py:8
  95.2 93.0 %collective-permute-start.1 = (f32[2,64,64,128]{3,2,1,0:T(8,128)S(1)}, f32[2,64,64,128]{3,2,1,0:T(8,128)}, u32[]{:S(2)}, u32[]{:S(2)}) collective-permute-start(f32[2,64,64,128]{3,2,1,0:T(8,128)S(1)} %fusion.39), channel_id=1, source_target_pairs={{0,2},{1,3},{2,0},{3,1},{4,6},{5,7},{6,4},{7,5},{8,10},{9,11},{10,... | collective-permute-start | bytes 12582920 | tf_op jit(solution)/shard_map/ppermute | solution.py:8
  197.5 94.1 %collective-permute-start.2 = (f32[2,64,64,128]{3,2,1,0:T(8,128)S(1)}, f32[2,64,64,128]{3,2,1,0:T(8,128)}, u32[]{:S(2)}, u32[]{:S(2)}) collective-permute-start(f32[2,64,64,128]{3,2,1,0:T(8,128)S(1)} %fusion.34), channel_id=1, source_target_pairs={{0,4},{1,5},{2,6},{3,7},{4,0},{5,1},{6,2},{7,3},{8,12},{9,13},{10,... | collective-permute-start | bytes 12582920 | tf_op jit(solution)/shard_map/ppermute | solution.py:8
  301.0 91.2 %collective-permute-start.3 = (f32[2,64,64,128]{3,2,1,0:T(8,128)S(1)}, f32[2,64,64,128]{3,2,1,0:T(8,128)S(1)}, u32[]{:S(2)}, u32[]{:S(2)}) collective-permute-start(f32[2,64,64,128]{3,2,1,0:T(8,128)S(1)} %fusion.29), channel_id=1, source_target_pairs={{0,8},{1,9},{2,10},{3,11},{4,12},{5,13},{6,14},{7,15},{8,0},{9,1},... | collective-permute-start | bytes 12582920 | tf_op jit(solution)/shard_map/ppermute | solution.py:8
where the time goes:
time: 401 us
  waiting for transfers between devices  278 us (69%)
  blocking collectives  58 us (14%)
  matrix products  37.3 us (9%)
  local copies, waits for them, and re-layouts  16.1 us (4%)
  starting transfers between devices  7.33 us (2%)
    ppermute x4, waiting for transfers between devices, partner(): lax.ppermute(x, axis, [(i, i ^ 1 << bit) for i in range(lax.axis_size(axi...  278 us
    all_to_all x1, blocking collectives, on_device(): lax.all_to_all(ordered, 'ma', split_axis=0, concat_axis=1, tiled=True)  58 us
    dot_general x4, matrix products, level_product(): lax.dot_general(factor_now, stacked, dims, precision=lax.Precision.HIGHES...  37.3 us
  transfers between devices with their start and end apart: 4, of which 4 were waited for; matrix products, arithmetic and copies ran while one was open for 0% of the time, Pallas kernels for 0%

commit v1 on v0

v1 whole, which is shorter than its diff:
```python
import functools

import jax
import jax.numpy as jnp
from jax import lax
from jax.experimental import pallas as pl
from jax.experimental.pallas import tpu as pltpu
from jax.sharding import PartitionSpec as P


def permute_xor(x, axis, mask):
    return lax.ppermute(x, axis, [(i, i ^ mask) for i in range(lax.axis_size(axis))])


def pick_body(place, owner_map, rows, out):
    del place, owner_map
    out[0] = rows[...]


def pick_slots(place, owner_map, rows, part, local_slots, block_cols):
    cycle_count = rows.shape[0]

    def column(slot, place, owner_map):
        return 0, owner_map[(place[0] ^ part) * local_slots + slot]

    return pl.pallas_call(
        pick_body,
        grid_spec=pltpu.PrefetchScalarGridSpec(
            num_scalar_prefetch=2,
            grid=(local_slots,),
            in_specs=[pl.BlockSpec((cycle_count, block_cols), column)],
            out_specs=pl.BlockSpec(
                (1, cycle_count, block_cols), lambda slot, place, owner_map: (slot, 0, 0)
            ),
        ),
        out_shape=jax.ShapeDtypeStruct((local_slots, cycle_count, block_cols), rows.dtype),
        cost_estimate=pl.CostEstimate(
            flops=0, bytes_accessed=8 * local_slots * cycle_count * block_cols, transcendentals=0
        ),
        name="pick_slots",
    )(place, owner_map, rows)


def split(x):
    high = x.astype(jnp.bfloat16)
    return high, (x - high.astype(jnp.float32)).astype(jnp.bfloat16)


def block_product(factor, own, other):
    factor_high, factor_low = split(factor)
    high, low = split(jnp.concatenate([own, other], axis=0))
    dot = functools.partial(jnp.dot, preferred_element_type=jnp.float32)
    return dot(factor_high, high) + (dot(factor_high, low) + dot(factor_low, high))


def level_body(place, factors, own, other, *refs):
    del place
    out = refs[-1]
    for group in range(own.shape[1]):
        out[0, group] = block_product(factors[0, 0, group], own[0, group], other[0, group])


def level_product(place, factors, own, other, level, part, filled=None, whole=False):
    slots, groups, rank, cols = own.shape
    step = 4
    per = groups // step
    block = (1, step, rank, cols)

    def local(slot, g, place):
        return slot, g, 0, 0

    def placed(slot, g, place):
        return slot, (place[0] ^ part) * per + g, 0, 0

    operands = [place, factors, own, other]
    in_specs = [
        pl.BlockSpec(
            (1, 1, step, rank, factors.shape[-1]),
            lambda slot, g, place: (level,) + placed(slot, g, place),
        ),
        pl.BlockSpec(block, local),
        pl.BlockSpec(block, local),
    ]
    aliases = {}
    if filled is not None:
        operands.append(filled)
        in_specs.append(pl.BlockSpec(memory_space=pl.ANY))
        aliases = {4: 0}
    shape = (slots, factors.shape[2], rank, cols) if whole else own.shape
    size = slots * groups * rank * cols
    return pl.pallas_call(
        level_body,
        grid_spec=pltpu.PrefetchScalarGridSpec(
            num_scalar_prefetch=1,
            grid=(slots, per),
            in_specs=in_specs,
            out_specs=pl.BlockSpec(block, placed if whole else local),
        ),
        out_shape=jax.ShapeDtypeStruct(shape, own.dtype),
        input_output_aliases=aliases,
        cost_estimate=pl.CostEstimate(
            flops=3 * 2 * size * factors.shape[-1], bytes_accessed=16 * size, transcendentals=0
        ),
        name="level_product",
    )(*operands)


def on_device(cycle_rows, owner_map, factors):
    block_count = owner_map.shape[0]
    block_cols = cycle_rows.shape[1] // block_count
    level_count, local_slots, group_count, rank, _ = factors.shape
    parts = lax.axis_size("ma")
    bit_count = lax.axis_size("blk").bit_length() - 1
    place = jnp.reshape(lax.axis_index("ma"), (1,)).astype(jnp.int32)
    part_shape = (local_slots, group_count // parts, rank, block_cols)
    coeffs = None
    for part in range(parts):
        state = pick_slots(place, owner_map, cycle_rows, part, local_slots, block_cols)
        if part:
            state = permute_xor(state, "ma", part)
        state = state.reshape(part_shape)
        for level in range(level_count):
            other = permute_xor(state, "blk", 1 << (level % bit_count))
            last = level == level_count - 1
            state = level_product(
                place, factors, state, other, level, part, coeffs if last else None, last
            )
        coeffs = state
    return coeffs


def solution(mesh):
    placed = (P(("ma", "blk"), None), P(), P(None, "ma", "blk", None, None))
    return jax.shard_map(
        on_device, mesh=mesh, in_specs=placed, out_specs=P("ma", "blk", None, None), check_vma=False
    )
```

time: 401 us -> 304 us (0.76)
  waiting for transfers between devices: 278 us -> 103 us
  Pallas kernels: 0 us -> 143 us
  blocking collectives: 58 us -> 0 us
  starting transfers between devices: 7.33 us -> 50.9 us
  matrix products: 37.3 us -> 0 us
  local copies, waits for them, and re-layouts: 16.1 us -> 4.95 us
    ppermute x4 -> x39, waiting for transfers between devices: 278 us -> 103 us  [permute_xor(): lax.ppermute(x, axis, [(i, i ^ mask) for i in range(lax.axis_size(axis))])]
    pallas_call x0 -> x40, Pallas kernels: none -> 143 us  [the longest x32 124 us: level_product(): pl.pallas_call(level_body, grid_spec=pltpu.PrefetchScalarGridSpec(num_sca...]
    all_to_all x1 -> x0, blocking collectives: 58 us -> none  [on_device(): lax.all_to_all(ordered, 'ma', split_axis=0, concat_axis=1, tiled=True)]
    ppermute x4 -> x39, starting transfers between devices: 7.33 us -> 50.9 us  [permute_xor(): lax.ppermute(x, axis, [(i, i ^ mask) for i in range(lax.axis_size(axis))])]
    dot_general x4 -> x0, matrix products: 37.3 us -> none  [level_product(): lax.dot_general(factor_now, stacked, dims, precision=lax.Precision.HIGHES...]
    reshape x1 -> x0, local copies, waits for them, and re-layouts: 5.34 us -> none  [slot_order(): rows.reshape(cycle_count, block_count, block_cols)]
    gather x1 -> x0, local copies, waits for them, and re-layouts: 5.01 us -> none  [slot_order(): return jnp.take(blocks, owner_map, axis=0)]
  transfers between devices with their start and end apart: 4 -> 39, of which waited for: 4 -> 15; matrix products, arithmetic and copies ran while one was open for 0% -> 0% of each run, Pallas kernels for 0% -> 45%
where the time goes in v1:
time: 304 us; the launch traced here: 302 us
  Pallas kernels  143 us (47%)
  waiting for transfers between devices  103 us (34%)
  starting transfers between devices  50.9 us (17%)
  local copies, waits for them, and re-layouts  4.95 us (2%)
    pallas_call x32, Pallas kernels, level_product(): pl.pallas_call(level_body, grid_spec=pltpu.PrefetchScalarGridSpec(num_sca...  124 us
    ppermute x39, waiting for transfers between devices, permute_xor(): lax.ppermute(x, axis, [(i, i ^ mask) for i in range(lax.axis_size(axis))])  103 us
    ppermute x39, starting transfers between devices, permute_xor(): lax.ppermute(x, axis, [(i, i ^ mask) for i in range(lax.axis_size(axis))])  50.9 us
    pallas_call x8, Pallas kernels, pick_slots(): pl.pallas_call(pick_body, grid_spec=pltpu.PrefetchScalarGridSpec(num_scal...  19.6 us
  transfers between devices with their start and end apart: 39, of which 15 were waited for; matrix products, arithmetic and copies ran while one was open for 0% of the time, Pallas kernels for 45%

profile of v1, /device:TPU:0, one launch (start us, length us, event | category | flops | bytes accessed | tf_op | source)
XLA Modules:
  0.0 302.0 jit_solution(18019645359307445087)
XLA Ops:
  33.8 14.1 %collective-permute-done.25 = f32[2,512,128]{2,1,0:T(8,128)S(1)} collective-permute-done((f32[2,512,128]{2,1,0:T(8,128)}, f32[2,512,128]{2,1,0:T(8,128)S(1)}, u32[]{:S(2)}, u32[]{:S(2)}) %collective-permute-start.25) | collective-permute-done | bytes 524320 | tf_op jit(solution)/shard_map/ppermute | solution.py:12
  50.9 3.9 %level_product.53.own = f32[2,8,64,128]{3,2,1,0:T(8,128)} custom-call(s32[1]{0:T(128)} %bitcast.place, f32[4,2,64,64,128]{4,3,2,1,0:T(8,128)} %factors.63, f32[2,8,64,128]{3,2,1,0:T(8,128)} %bitcast.10, f32[2,8,64,128]{3,2,1,0:T(8,128)} %copy-done.31), custom_call_target="tpu_custom_call" | custom-call | flops 100663296 | bytes 2097152 | tf_op jit(solution)/shard_map/level_product/pallas_call | solution.py:91
  56.7 15.5 %collective-permute-done.15 = f32[2,512,128]{2,1,0:T(8,128)S(1)} collective-permute-done((f32[2,512,128]{2,1,0:T(8,128)}, f32[2,512,128]{2,1,0:T(8,128)S(1)}, u32[]{:S(2)}, u32[]{:S(2)}) %collective-permute-start.15) | collective-permute-done | bytes 524320 | tf_op jit(solution)/shard_map/ppermute | solution.py:12
  72.8 3.6 %collective-permute-done.5 = f32[2,512,128]{2,1,0:T(8,128)S(1)} collective-permute-done((f32[2,512,128]{2,1,0:T(8,128)}, f32[2,512,128]{2,1,0:T(8,128)S(1)}, u32[]{:S(2)}, u32[]{:S(2)}) %collective-permute-start.5) | collective-permute-done | bytes 524320 | tf_op jit(solution)/shard_map/ppermute | solution.py:12
  78.5 3.9 %level_product.54.own = f32[2,8,64,128]{3,2,1,0:T(8,128)} custom-call(s32[1]{0:T(128)} %bitcast.place, f32[4,2,64,64,128]{4,3,2,1,0:T(8,128)} %factors.63, f32[2,8,64,128]{3,2,1,0:T(8,128)} %level_product.53.own, f32[2,8,64,128]{3,2,1,0:T(8,128)} %copy-done.30), custom_call_target="tpu_custom_call" | custom-call | flops 100663296 | bytes 2097152 | tf_op jit(solution)/shard_map/level_product/pallas_call | solution.py:91
  82.4 4.0 %collective-permute-start.37 = (f32[2,8,64,128]{3,2,1,0:T(8,128)}, f32[2,8,64,128]{3,2,1,0:T(8,128)S(1)}, u32[]{:S(2)}, u32[]{:S(2)}) collective-permute-start(f32[2,8,64,128]{3,2,1,0:T(8,128)} %level_product.54.own), channel_id=1, source_target_pairs={{0,4},{1,5},{2,6},{3,7},{4,0},{5,1},{6,2},{7,3},{8,12},{9,13},{10,... | collective-permute-start | bytes 1572872 | tf_op jit(solution)/shard_map/ppermute | solution.py:12
  86.4 3.9 %level_product.50.own = f32[2,8,64,128]{3,2,1,0:T(8,128)} custom-call(s32[1]{0:T(128)} %bitcast.place, f32[4,2,64,64,128]{4,3,2,1,0:T(8,128)} %factors.63, f32[2,8,64,128]{3,2,1,0:T(8,128)} %bitcast.24, f32[2,8,64,128]{3,2,1,0:T(8,128)} %copy-done.29), custom_call_target="tpu_custom_call" | custom-call | flops 100663296 | bytes 2097152 | tf_op jit(solution)/shard_map/level_product/pallas_call | solution.py:91
  91.3 3.8 %level_product.47.own = f32[2,8,64,128]{3,2,1,0:T(8,128)} custom-call(s32[1]{0:T(128)} %bitcast.place, f32[4,2,64,64,128]{4,3,2,1,0:T(8,128)} %factors.63, f32[2,8,64,128]{3,2,1,0:T(8,128)} %bitcast.22, f32[2,8,64,128]{3,2,1,0:T(8,128)} %copy-done.28), custom_call_target="tpu_custom_call" | custom-call | flops 100663296 | bytes 2097152 | tf_op jit(solution)/shard_map/level_product/pallas_call | solution.py:91
  96.1 3.9 %level_product.44.own = f32[2,8,64,128]{3,2,1,0:T(8,128)} custom-call(s32[1]{0:T(128)} %bitcast.place, f32[4,2,64,64,128]{4,3,2,1,0:T(8,128)} %factors.63, f32[2,8,64,128]{3,2,1,0:T(8,128)} %bitcast.20, f32[2,8,64,128]{3,2,1,0:T(8,128)} %collective-permute-done.21.other), custom_call_target="tpu_custom_call" | custom-call | flops 100663296 | bytes 2097152 | tf_op jit(solution)/shard_map/level_product/pallas_call | solution.py:91
  101.0 3.9 %level_product.41.own = f32[2,8,64,128]{3,2,1,0:T(8,128)} custom-call(s32[1]{0:T(128)} %bitcast.place, f32[4,2,64,64,128]{4,3,2,1,0:T(8,128)} %factors.63, f32[2,8,64,128]{3,2,1,0:T(8,128)} %bitcast.18, f32[2,8,64,128]{3,2,1,0:T(8,128)} %collective-permute-done.16.other), custom_call_target="tpu_custom_call" | custom-call | flops 100663296 | bytes 2097152 | tf_op jit(solution)/shard_map/level_product/pallas_call | solution.py:91
  106.0 3.9 %level_product.38.own = f32[2,8,64,128]{3,2,1,0:T(8,128)} custom-call(s32[1]{0:T(128)} %bitcast.place, f32[4,2,64,64,128]{4,3,2,1,0:T(8,128)} %factors.63, f32[2,8,64,128]{3,2,1,0:T(8,128)} %bitcast.16, f32[2,8,64,128]{3,2,1,0:T(8,128)} %collective-permute-done.11.other), custom_call_target="tpu_custom_call" | custom-call | flops 100663296 | bytes 2097152 | tf_op jit(solution)/shard_map/level_product/pallas_call | solution.py:91
  111.0 3.9 %level_product.35.own = f32[2,8,64,128]{3,2,1,0:T(8,128)} custom-call(s32[1]{0:T(128)} %bitcast.place, f32[4,2,64,64,128]{4,3,2,1,0:T(8,128)} %factors.63, f32[2,8,64,128]{3,2,1,0:T(8,128)} %bitcast.14, f32[2,8,64,128]{3,2,1,0:T(8,128)} %collective-permute-done.6.other), custom_call_target="tpu_custom_call" | custom-call | flops 100663296 | bytes 2097152 | tf_op jit(solution)/shard_map/level_product/pallas_call | solution.py:91
  115.9 3.9 %level_product.32.own = f32[2,8,64,128]{3,2,1,0:T(8,128)} custom-call(s32[1]{0:T(128)} %bitcast.place, f32[4,2,64,64,128]{4,3,2,1,0:T(8,128)} %factors.63, f32[2,8,64,128]{3,2,1,0:T(8,128)} %bitcast.12, f32[2,8,64,128]{3,2,1,0:T(8,128)} %copy-done.15), custom_call_target="tpu_custom_call" | custom-call | flops 100663296 | bytes 2097152 | tf_op jit(solution)/shard_map/level_product/pallas_call | solution.py:91
  123.8 3.9 %level_product.55.own = f32[2,8,64,128]{3,2,1,0:T(8,128)} custom-call(s32[1]{0:T(128)} %bitcast.place, f32[4,2,64,64,128]{4,3,2,1,0:T(8,128)} %factors.63, f32[2,8,64,128]{3,2,1,0:T(8,128)} %level_product.54.own, f32[2,8,64,128]{3,2,1,0:T(8,128)} %copy-done.16), custom_call_target="tpu_custom_call" | custom-call | flops 100663296 | bytes 2097152 | tf_op jit(solution)/shard_map/level_product/pallas_call | solution.py:91
  127.7 6.4 %collective-permute-done.22.other = f32[2,8,64,128]{3,2,1,0:T(8,128)S(1)} collective-permute-done((f32[2,8,64,128]{3,2,1,0:T(8,128)}, f32[2,8,64,128]{3,2,1,0:T(8,128)S(1)}, u32[]{:S(2)}, u32[]{:S(2)}) %collective-permute-start.22) | collective-permute-done | bytes 524320 | tf_op jit(solution)/shard_map/ppermute | solution.py:12
  134.6 3.9 %level_product.51.own = f32[2,8,64,128]{3,2,1,0:T(8,128)} custom-call(s32[1]{0:T(128)} %bitcast.place, f32[4,2,64,64,128]{4,3,2,1,0:T(8,128)} %factors.63, f32[2,8,64,128]{3,2,1,0:T(8,128)} %level_product.50.own, f32[2,8,64,128]{3,2,1,0:T(8,128)} %copy-done.17), custom_call_target="tpu_custom_call" | custom-call | flops 100663296 | bytes 2097152 | tf_op jit(solution)/shard_map/level_product/pallas_call | solution.py:91
  138.5 6.9 %collective-permute-done.17.other = f32[2,8,64,128]{3,2,1,0:T(8,128)} collective-permute-done((f32[2,8,64,128]{3,2,1,0:T(8,128)}, f32[2,8,64,128]{3,2,1,0:T(8,128)}, u32[]{:S(2)}, u32[]{:S(2)}) %collective-permute-start.17) | collective-permute-done | bytes 524320 | tf_op jit(solution)/shard_map/ppermute | solution.py:12
  146.5 3.9 %level_product.48.own = f32[2,8,64,128]{3,2,1,0:T(8,128)} custom-call(s32[1]{0:T(128)} %bitcast.place, f32[4,2,64,64,128]{4,3,2,1,0:T(8,128)} %factors.63, f32[2,8,64,128]{3,2,1,0:T(8,128)} %level_product.47.own, f32[2,8,64,128]{3,2,1,0:T(8,128)} %copy-done.18), custom_call_target="tpu_custom_call" | custom-call | flops 100663296 | bytes 2097152 | tf_op jit(solution)/shard_map/level_product/pallas_call | solution.py:91
  150.4 6.1 %collective-permute-done.12.other = f32[2,8,64,128]{3,2,1,0:T(8,128)S(1)} collective-permute-done((f32[2,8,64,128]{3,2,1,0:T(8,128)}, f32[2,8,64,128]{3,2,1,0:T(8,128)S(1)}, u32[]{:S(2)}, u32[]{:S(2)}) %collective-permute-start.12) | collective-permute-done | bytes 524320 | tf_op jit(solution)/shard_map/ppermute | solution.py:12
  157.7 3.8 %level_product.45.own = f32[2,8,64,128]{3,2,1,0:T(8,128)} custom-call(s32[1]{0:T(128)} %bitcast.place, f32[4,2,64,64,128]{4,3,2,1,0:T(8,128)} %factors.63, f32[2,8,64,128]{3,2,1,0:T(8,128)} %level_product.44.own, f32[2,8,64,128]{3,2,1,0:T(8,128)} %copy-done.19), custom_call_target="tpu_custom_call" | custom-call | flops 100663296 | bytes 2097152 | tf_op jit(solution)/shard_map/level_product/pallas_call | solution.py:91
  161.5 6.2 %collective-permute-done.7.other = f32[2,8,64,128]{3,2,1,0:T(8,128)S(1)} collective-permute-done((f32[2,8,64,128]{3,2,1,0:T(8,128)}, f32[2,8,64,128]{3,2,1,0:T(8,128)S(1)}, u32[]{:S(2)}, u32[]{:S(2)}) %collective-permute-start.7) | collective-permute-done | bytes 524320 | tf_op jit(solution)/shard_map/ppermute | solution.py:12
  168.9 3.9 %level_product.42.own = f32[2,8,64,128]{3,2,1,0:T(8,128)} custom-call(s32[1]{0:T(128)} %bitcast.place, f32[4,2,64,64,128]{4,3,2,1,0:T(8,128)} %factors.63, f32[2,8,64,128]{3,2,1,0:T(8,128)} %level_product.41.own, f32[2,8,64,128]{3,2,1,0:T(8,128)} %collective-permute-done.17.other), custom_call_target="tpu_custom_call" | custom-call | flops 100663296 | bytes 2097152 | tf_op jit(solution)/shard_map/level_product/pallas_call | solution.py:91
  172.8 6.2 %collective-permute-done.2.other = f32[2,8,64,128]{3,2,1,0:T(8,128)S(1)} collective-permute-done((f32[2,8,64,128]{3,2,1,0:T(8,128)}, f32[2,8,64,128]{3,2,1,0:T(8,128)S(1)}, u32[]{:S(2)}, u32[]{:S(2)}) %collective-permute-start.2) | collective-permute-done | bytes 524320 | tf_op jit(solution)/shard_map/ppermute | solution.py:12
  180.1 3.9 %level_product.39.own = f32[2,8,64,128]{3,2,1,0:T(8,128)} custom-call(s32[1]{0:T(128)} %bitcast.place, f32[4,2,64,64,128]{4,3,2,1,0:T(8,128)} %factors.63, f32[2,8,64,128]{3,2,1,0:T(8,128)} %level_product.38.own, f32[2,8,64,128]{3,2,1,0:T(8,128)} %copy-done.20), custom_call_target="tpu_custom_call" | custom-call | flops 100663296 | bytes 2097152 | tf_op jit(solution)/shard_map/level_product/pallas_call | solution.py:91
  186.4 3.9 %level_product.36.own = f32[2,8,64,128]{3,2,1,0:T(8,128)} custom-call(s32[1]{0:T(128)} %bitcast.place, f32[4,2,64,64,128]{4,3,2,1,0:T(8,128)} %factors.63, f32[2,8,64,128]{3,2,1,0:T(8,128)} %level_product.35.own, f32[2,8,64,128]{3,2,1,0:T(8,128)} %copy-done.21), custom_call_target="tpu_custom_call" | custom-call | flops 100663296 | bytes 2097152 | tf_op jit(solution)/shard_map/level_product/pallas_call | solution.py:91
  192.7 3.9 %level_product.33.own = f32[2,8,64,128]{3,2,1,0:T(8,128)} custom-call(s32[1]{0:T(128)} %bitcast.place, f32[4,2,64,64,128]{4,3,2,1,0:T(8,128)} %factors.63, f32[2,8,64,128]{3,2,1,0:T(8,128)} %level_product.32.own, f32[2,8,64,128]{3,2,1,0:T(8,128)} %copy-done.22), custom_call_target="tpu_custom_call" | custom-call | flops 100663296 | bytes 2097152 | tf_op jit(solution)/shard_map/level_product/pallas_call | solution.py:91
  196.6 3.8 %collective-permute-done.28.other = f32[2,8,64,128]{3,2,1,0:T(8,128)S(1)} collective-permute-done((f32[2,8,64,128]{3,2,1,0:T(8,128)}, f32[2,8,64,128]{3,2,1,0:T(8,128)S(1)}, u32[]{:S(2)}, u32[]{:S(2)}) %collective-permute-start.28) | collective-permute-done | bytes 524320 | tf_op jit(solution)/shard_map/ppermute | solution.py:12
  200.4 3.6 %collective-permute-start.3 = (f32[2,8,64,128]{3,2,1,0:T(8,128)}, f32[2,8,64,128]{3,2,1,0:T(8,128)}, u32[]{:S(2)}, u32[]{:S(2)}) collective-permute-start(f32[2,8,64,128]{3,2,1,0:T(8,128)} %level_product.33.own), channel_id=1, source_target_pairs={{0,4},{1,5},{2,6},{3,7},{4,0},{5,1},{6,2},{7,3},{8,12},{9,13},{10,... | collective-permute-start | bytes 1572872 | tf_op jit(solution)/shard_map/ppermute | solution.py:12
  204.0 3.9 %level_product.52.own = f32[2,8,64,128]{3,2,1,0:T(8,128)} custom-call(s32[1]{0:T(128)} %bitcast.place, f32[4,2,64,64,128]{4,3,2,1,0:T(8,128)} %factors.63, f32[2,8,64,128]{3,2,1,0:T(8,128)} %level_product.51.own, f32[2,8,64,128]{3,2,1,0:T(8,128)} %copy-done.23), custom_call_target="tpu_custom_call" | custom-call | flops 100663296 | bytes 2097152 | tf_op jit(solution)/shard_map/level_product/pallas_call | solution.py:91
  207.8 3.8 %collective-permute-done.23.other = f32[2,8,64,128]{3,2,1,0:T(8,128)S(1)} collective-permute-done((f32[2,8,64,128]{3,2,1,0:T(8,128)}, f32[2,8,64,128]{3,2,1,0:T(8,128)S(1)}, u32[]{:S(2)}, u32[]{:S(2)}) %collective-permute-start.23) | collective-permute-done | bytes 524320 | tf_op jit(solution)/shard_map/ppermute | solution.py:12
  212.2 3.9 %level_product.49.own = f32[2,8,64,128]{3,2,1,0:T(8,128)} custom-call(s32[1]{0:T(128)} %bitcast.place, f32[4,2,64,64,128]{4,3,2,1,0:T(8,128)} %factors.63, f32[2,8,64,128]{3,2,1,0:T(8,128)} %level_product.48.own, f32[2,8,64,128]{3,2,1,0:T(8,128)} %copy-done.24), custom_call_target="tpu_custom_call" | custom-call | flops 100663296 | bytes 2097152 | tf_op jit(solution)/shard_map/level_product/pallas_call | solution.py:91
  216.1 6.8 %collective-permute-done.18.other = f32[2,8,64,128]{3,2,1,0:T(8,128)S(1)} collective-permute-done((f32[2,8,64,128]{3,2,1,0:T(8,128)}, f32[2,8,64,128]{3,2,1,0:T(8,128)S(1)}, u32[]{:S(2)}, u32[]{:S(2)}) %collective-permute-start.18) | collective-permute-done | bytes 524320 | tf_op jit(solution)/shard_map/ppermute | solution.py:12
  223.5 3.9 %level_product.46.own = f32[2,8,64,128]{3,2,1,0:T(8,128)} custom-call(s32[1]{0:T(128)} %bitcast.place, f32[4,2,64,64,128]{4,3,2,1,0:T(8,128)} %factors.63, f32[2,8,64,128]{3,2,1,0:T(8,128)} %level_product.45.own, f32[2,8,64,128]{3,2,1,0:T(8,128)} %copy-done.25), custom_call_target="tpu_custom_call" | custom-call | flops 100663296 | bytes 2097152 | tf_op jit(solution)/shard_map/level_product/pallas_call | solution.py:91
  227.3 6.8 %collective-permute-done.13.other = f32[2,8,64,128]{3,2,1,0:T(8,128)S(1)} collective-permute-done((f32[2,8,64,128]{3,2,1,0:T(8,128)}, f32[2,8,64,128]{3,2,1,0:T(8,128)S(1)}, u32[]{:S(2)}, u32[]{:S(2)}) %collective-permute-start.13) | collective-permute-done | bytes 524320 | tf_op jit(solution)/shard_map/ppermute | solution.py:12
  234.7 3.9 %level_product.43.own = f32[2,8,64,128]{3,2,1,0:T(8,128)} custom-call(s32[1]{0:T(128)} %bitcast.place, f32[4,2,64,64,128]{4,3,2,1,0:T(8,128)} %factors.63, f32[2,8,64,128]{3,2,1,0:T(8,128)} %level_product.42.own, f32[2,8,64,128]{3,2,1,0:T(8,128)} %copy-done.26), custom_call_target="tpu_custom_call" | custom-call | flops 100663296 | bytes 2097152 | tf_op jit(solution)/shard_map/level_product/pallas_call | solution.py:91
  238.6 6.9 %collective-permute-done.8.other = f32[2,8,64,128]{3,2,1,0:T(8,128)} collective-permute-done((f32[2,8,64,128]{3,2,1,0:T(8,128)}, f32[2,8,64,128]{3,2,1,0:T(8,128)}, u32[]{:S(2)}, u32[]{:S(2)}) %collective-permute-start.8) | collective-permute-done | bytes 524320 | tf_op jit(solution)/shard_map/ppermute | solution.py:12
  246.0 3.8 %level_product.40.own = f32[2,8,64,128]{3,2,1,0:T(8,128)} custom-call(s32[1]{0:T(128)} %bitcast.place, f32[4,2,64,64,128]{4,3,2,1,0:T(8,128)} %factors.63, f32[2,8,64,128]{3,2,1,0:T(8,128)} %level_product.39.own, f32[2,8,64,128]{3,2,1,0:T(8,128)} %copy-done.27), custom_call_target="tpu_custom_call" | custom-call | flops 100663296 | bytes 2097152 | tf_op jit(solution)/shard_map/level_product/pallas_call | solution.py:91
  249.9 6.5 %collective-permute-done.3.other = f32[2,8,64,128]{3,2,1,0:T(8,128)} collective-permute-done((f32[2,8,64,128]{3,2,1,0:T(8,128)}, f32[2,8,64,128]{3,2,1,0:T(8,128)}, u32[]{:S(2)}, u32[]{:S(2)}) %collective-permute-start.3) | collective-permute-done | bytes 524320 | tf_op jit(solution)/shard_map/ppermute | solution.py:12
  257.0 3.9 %level_product.37.own = f32[2,8,64,128]{3,2,1,0:T(8,128)} custom-call(s32[1]{0:T(128)} %bitcast.place, f32[4,2,64,64,128]{4,3,2,1,0:T(8,128)} %factors.63, f32[2,8,64,128]{3,2,1,0:T(8,128)} %level_product.36.own, f32[2,8,64,128]{3,2,1,0:T(8,128)} %collective-permute-done.8.other), custom_call_target="tpu_custom_call" | custom-call | flops 100663296 | bytes 2097152 | tf_op jit(solution)/shard_map/level_product/pallas_call | solution.py:91
  262.4 3.9 %level_product.34.own = f32[2,8,64,128]{3,2,1,0:T(8,128)} custom-call(s32[1]{0:T(128)} %bitcast.place, f32[4,2,64,64,128]{4,3,2,1,0:T(8,128)} %factors.63, f32[2,8,64,128]{3,2,1,0:T(8,128)} %level_product.33.own, f32[2,8,64,128]{3,2,1,0:T(8,128)} %collective-permute-done.3.other), custom_call_target="tpu_custom_call" | custom-call | flops 100663296 | bytes 2097152 | tf_op jit(solution)/shard_map/level_product/pallas_call | solution.py:91
  267.0 3.9 %level_product.56.refs_0_ = f32[2,64,64,128]{3,2,1,0:T(8,128)} custom-call(s32[1]{0:T(128)} %bitcast.place, f32[4,2,64,64,128]{4,3,2,1,0:T(8,128)} %factors.63, f32[2,8,64,128]{3,2,1,0:T(8,128)} %level_product.55.own, f32[2,8,64,128]{3,2,1,0:T(8,128)} %copy-done), custom_call_target="tpu_custom_call" | custom-call | flops 100663296 | bytes 2097152 | tf_op jit(solution)/shard_map/level_product/pallas_call | solution.py:91
  270.8 3.9 %level_product.57.refs_0_ = f32[2,64,64,128]{3,2,1,0:T(8,128)} custom-call(s32[1]{0:T(128)} %bitcast.place, f32[4,2,64,64,128]{4,3,2,1,0:T(8,128)} %factors.63, f32[2,8,64,128]{3,2,1,0:T(8,128)} %level_product.52.own, f32[2,8,64,128]{3,2,1,0:T(8,128)} %copy-done.1, f32[2,64,64,128]{3,2,1,0:T(8,128)} %level_product.56.refs_0_), custom_call_target="tpu_custom_call", output_to_operand_aliasing={{}: (4, {})} | custom-call | flops 100663296 | bytes 2097152 | tf_op jit(solution)/shard_map/level_product/pallas_call | solution.py:91
  274.7 3.9 %level_product.58.refs_0_ = f32[2,64,64,128]{3,2,1,0:T(8,128)} custom-call(s32[1]{0:T(128)} %bitcast.place, f32[4,2,64,64,128]{4,3,2,1,0:T(8,128)} %factors.63, f32[2,8,64,128]{3,2,1,0:T(8,128)} %level_product.49.own, f32[2,8,64,128]{3,2,1,0:T(8,128)} %copy-done.2, f32[2,64,64,128]{3,2,1,0:T(8,128)} %level_product.57.refs_0_), custom_call_target="tpu_custom_call", output_to_operand_aliasing={{}: (4, {})} | custom-call | flops 100663296 | bytes 2097152 | tf_op jit(solution)/shard_map/level_product/pallas_call | solution.py:91
  279.4 3.9 %level_product.59.refs_0_ = f32[2,64,64,128]{3,2,1,0:T(8,128)} custom-call(s32[1]{0:T(128)} %bitcast.place, f32[4,2,64,64,128]{4,3,2,1,0:T(8,128)} %factors.63, f32[2,8,64,128]{3,2,1,0:T(8,128)} %level_product.46.own, f32[2,8,64,128]{3,2,1,0:T(8,128)} %copy-done.3, f32[2,64,64,128]{3,2,1,0:T(8,128)} %level_product.58.refs_0_), custom_call_target="tpu_custom_call", output_to_operand_aliasing={{}: (4, {})} | custom-call | flops 100663296 | bytes 2097152 | tf_op jit(solution)/shard_map/level_product/pallas_call | solution.py:91
  284.1 3.9 %level_product.60.refs_0_ = f32[2,64,64,128]{3,2,1,0:T(8,128)} custom-call(s32[1]{0:T(128)} %bitcast.place, f32[4,2,64,64,128]{4,3,2,1,0:T(8,128)} %factors.63, f32[2,8,64,128]{3,2,1,0:T(8,128)} %level_product.43.own, f32[2,8,64,128]{3,2,1,0:T(8,128)} %copy-done.4, f32[2,64,64,128]{3,2,1,0:T(8,128)} %level_product.59.refs_0_), custom_call_target="tpu_custom_call", output_to_operand_aliasing={{}: (4, {})} | custom-call | flops 100663296 | bytes 2097152 | tf_op jit(solution)/shard_map/level_product/pallas_call | solution.py:91
  288.7 3.9 %level_product.61.refs_0_ = f32[2,64,64,128]{3,2,1,0:T(8,128)} custom-call(s32[1]{0:T(128)} %bitcast.place, f32[4,2,64,64,128]{4,3,2,1,0:T(8,128)} %factors.63, f32[2,8,64,128]{3,2,1,0:T(8,128)} %level_product.40.own, f32[2,8,64,128]{3,2,1,0:T(8,128)} %copy-done.5, f32[2,64,64,128]{3,2,1,0:T(8,128)} %level_product.60.refs_0_), custom_call_target="tpu_custom_call", output_to_operand_aliasing={{}: (4, {})} | custom-call | flops 100663296 | bytes 2097152 | tf_op jit(solution)/shard_map/level_product/pallas_call | solution.py:91
  293.4 3.9 %level_product.62.refs_0_ = f32[2,64,64,128]{3,2,1,0:T(8,128)} custom-call(s32[1]{0:T(128)} %bitcast.place, f32[4,2,64,64,128]{4,3,2,1,0:T(8,128)} %factors.63, f32[2,8,64,128]{3,2,1,0:T(8,128)} %level_product.37.own, f32[2,8,64,128]{3,2,1,0:T(8,128)} %copy-done.6, f32[2,64,64,128]{3,2,1,0:T(8,128)} %level_product.61.refs_0_), custom_call_target="tpu_custom_call", output_to_operand_aliasing={{}: (4, {})} | custom-call | flops 100663296 | bytes 2097152 | tf_op jit(solution)/shard_map/level_product/pallas_call | solution.py:91
  298.1 3.9 %level_product.63 = f32[2,64,64,128]{3,2,1,0:T(8,128)} custom-call(s32[1]{0:T(128)} %bitcast.place, f32[4,2,64,64,128]{4,3,2,1,0:T(8,128)} %factors.63, f32[2,8,64,128]{3,2,1,0:T(8,128)} %level_product.34.own, f32[2,8,64,128]{3,2,1,0:T(8,128)} %copy-done.7, f32[2,64,64,128]{3,2,1,0:T(8,128)} %level_product.62.refs_0_), custom_call_target="tpu_custom_call", output_to_operand_aliasing={{}: (4, {})} | custom-call | flops 100663296 | bytes 2097152 | tf_op jit(solution)/shard_map/level_product/pallas_call | solution.py:91
  (134 shorter events, 71.0 us)
Async XLA Ops:
  2.5 20.5 %collective-permute-start.35 = (f32[2,8,64,128]{3,2,1,0:T(8,128)}, f32[2,8,64,128]{3,2,1,0:T(8,128)S(1)}, u32[]{:S(2)}, u32[]{:S(2)}) collective-permute-start(f32[2,8,64,128]{3,2,1,0:T(8,128)} %bitcast.9), channel_id=1, source_target_pairs={{0,1},{1,0},{2,3},{3,2},{4,5},{5,4},{6,7},{7,6},{8,9},{9,8},{10,11... | collective-permute-start | bytes 1572872 | tf_op jit(solution)/shard_map/ppermute | solution.py:12
  4.9 23.4 %collective-permute-start.30 = (f32[2,512,128]{2,1,0:T(8,128)}, f32[2,512,128]{2,1,0:T(8,128)S(1)}, u32[]{:S(2)}, u32[]{:S(2)}) collective-permute-start(f32[2,512,128]{2,1,0:T(8,128)} %pick_slots.14), channel_id=1, source_target_pairs={{0,16},{16,0},{32,48},{48,32},{64,80},{80,64},{96,112},{112,96},{1... | collective-permute-start | bytes 1572872 | tf_op jit(solution)/shard_map/ppermute | solution.py:12
  10.5 37.4 %collective-permute-start.25 = (f32[2,512,128]{2,1,0:T(8,128)}, f32[2,512,128]{2,1,0:T(8,128)S(1)}, u32[]{:S(2)}, u32[]{:S(2)}) collective-permute-start(f32[2,512,128]{2,1,0:T(8,128)} %pick_slots.13), channel_id=1, source_target_pairs={{0,32},{16,48},{32,0},{48,16},{64,96},{80,112},{96,64},{112,80},{1... | collective-permute-start | bytes 1572872 | tf_op jit(solution)/shard_map/ppermute | solution.py:12
  14.5 40.2 %collective-permute-start.20 = (f32[2,512,128]{2,1,0:T(8,128)}, f32[2,512,128]{2,1,0:T(8,128)S(1)}, u32[]{:S(2)}, u32[]{:S(2)}) collective-permute-start(f32[2,512,128]{2,1,0:T(8,128)} %pick_slots.12), channel_id=1, source_target_pairs={{0,48},{16,32},{32,16},{48,0},{64,112},{80,96},{96,80},{112,64},{1... | collective-permute-start | bytes 1572872 | tf_op jit(solution)/shard_map/ppermute | solution.py:12
  17.2 55.0 %collective-permute-start.15 = (f32[2,512,128]{2,1,0:T(8,128)}, f32[2,512,128]{2,1,0:T(8,128)S(1)}, u32[]{:S(2)}, u32[]{:S(2)}) collective-permute-start(f32[2,512,128]{2,1,0:T(8,128)} %pick_slots.11), channel_id=1, source_target_pairs={{0,64},{16,80},{32,96},{48,112},{64,0},{80,16},{96,32},{112,48},{1... | collective-permute-start | bytes 1572872 | tf_op jit(solution)/shard_map/ppermute | solution.py:12
  23.0 49.2 %collective-permute-start.10 = (f32[2,512,128]{2,1,0:T(8,128)}, f32[2,512,128]{2,1,0:T(8,128)S(1)}, u32[]{:S(2)}, u32[]{:S(2)}) collective-permute-start(f32[2,512,128]{2,1,0:T(8,128)} %pick_slots.10), channel_id=1, source_target_pairs={{0,80},{16,64},{32,112},{48,96},{64,16},{80,0},{96,48},{112,32},{1... | collective-permute-start | bytes 1572872 | tf_op jit(solution)/shard_map/ppermute | solution.py:12
  28.3 48.2 %collective-permute-start.5 = (f32[2,512,128]{2,1,0:T(8,128)}, f32[2,512,128]{2,1,0:T(8,128)S(1)}, u32[]{:S(2)}, u32[]{:S(2)}) collective-permute-start(f32[2,512,128]{2,1,0:T(8,128)} %pick_slots.9), channel_id=1, source_target_pairs={{0,96},{16,112},{32,64},{48,80},{64,32},{80,48},{96,0},{112,16},{1... | collective-permute-start | bytes 1572872 | tf_op jit(solution)/shard_map/ppermute | solution.py:12
  47.9 24.3 %copy-start.13 = (f32[2,512,128]{2,1,0:T(8,128)}, f32[2,512,128]{2,1,0:T(8,128)S(1)}, u32[]{:S(2)}) copy-start(f32[2,512,128]{2,1,0:T(8,128)S(1)} %collective-permute-done.25) | copy-start | bytes 1572868
  47.9 28.6 %collective-permute-start = (f32[2,512,128]{2,1,0:T(8,128)}, f32[2,512,128]{2,1,0:T(8,128)S(1)}, u32[]{:S(2)}, u32[]{:S(2)}) collective-permute-start(f32[2,512,128]{2,1,0:T(8,128)} %pick_slots.8), channel_id=1, source_target_pairs={{0,112},{16,96},{32,80},{48,64},{64,48},{80,32},{96,16},{112,0},{1... | collective-permute-start | bytes 1572872 | tf_op jit(solution)/shard_map/ppermute | solution.py:12
  54.7 27.7 %copy-start.12 = (f32[2,512,128]{2,1,0:T(8,128)}, f32[2,512,128]{2,1,0:T(8,128)S(1)}, u32[]{:S(2)}) copy-start(f32[2,512,128]{2,1,0:T(8,128)S(1)} %collective-permute-done.20) | copy-start | bytes 1572868
  54.7 22.3 %collective-permute-start.36 = (f32[2,8,64,128]{3,2,1,0:T(8,128)}, f32[2,8,64,128]{3,2,1,0:T(8,128)S(1)}, u32[]{:S(2)}, u32[]{:S(2)}) collective-permute-start(f32[2,8,64,128]{3,2,1,0:T(8,128)} %level_product.53.own), channel_id=1, source_target_pairs={{0,2},{1,3},{2,0},{3,1},{4,6},{5,7},{6,4},{7,5},{8,10},{9,11},{10,... | collective-permute-start | bytes 1572872 | tf_op jit(solution)/shard_map/ppermute | solution.py:12
  72.2 10.2 %copy-start.11 = (f32[2,512,128]{2,1,0:T(8,128)}, f32[2,512,128]{2,1,0:T(8,128)S(1)}, u32[]{:S(2)}) copy-start(f32[2,512,128]{2,1,0:T(8,128)S(1)} %collective-permute-done.15) | copy-start | bytes 1572868
  72.2 4.9 %collective-permute-start.31 = (f32[2,8,64,128]{3,2,1,0:T(8,128)}, f32[2,8,64,128]{3,2,1,0:T(8,128)S(1)}, u32[]{:S(2)}, u32[]{:S(2)}) collective-permute-start(f32[2,8,64,128]{3,2,1,0:T(8,128)} %bitcast.23), channel_id=1, source_target_pairs={{0,1},{1,0},{2,3},{3,2},{4,5},{5,4},{6,7},{7,6},{8,9},{9,8},{10,11... | collective-permute-start | bytes 1572872 | tf_op jit(solution)/shard_map/ppermute | solution.py:12
  72.2 10.2 %copy-start.10 = (f32[2,512,128]{2,1,0:T(8,128)}, f32[2,512,128]{2,1,0:T(8,128)S(1)}, u32[]{:S(2)}) copy-start(f32[2,512,128]{2,1,0:T(8,128)S(1)} %collective-permute-done.10) | copy-start | bytes 1572868
  72.2 5.3 %collective-permute-start.26 = (f32[2,8,64,128]{3,2,1,0:T(8,128)S(1)}, f32[2,8,64,128]{3,2,1,0:T(8,128)S(1)}, u32[]{:S(2)}, u32[]{:S(2)}) collective-permute-start(f32[2,8,64,128]{3,2,1,0:T(8,128)S(1)} %bitcast.21), channel_id=1, source_target_pairs={{0,1},{1,0},{2,3},{3,2},{4,5},{5,4},{6,7},{7,6},{8,9},{9,8},{10,11... | collective-permute-start | bytes 1572872 | tf_op jit(solution)/shard_map/ppermute | solution.py:12
  76.5 5.9 %copy-start.9 = (f32[2,512,128]{2,1,0:T(8,128)}, f32[2,512,128]{2,1,0:T(8,128)S(1)}, u32[]{:S(2)}) copy-start(f32[2,512,128]{2,1,0:T(8,128)S(1)} %collective-permute-done.5) | copy-start | bytes 1572868
  76.5 6.0 %collective-permute-start.21 = (f32[2,8,64,128]{3,2,1,0:T(8,128)S(1)}, f32[2,8,64,128]{3,2,1,0:T(8,128)}, u32[]{:S(2)}, u32[]{:S(2)}) collective-permute-start(f32[2,8,64,128]{3,2,1,0:T(8,128)S(1)} %bitcast.19), channel_id=1, source_target_pairs={{0,1},{1,0},{2,3},{3,2},{4,5},{5,4},{6,7},{7,6},{8,9},{9,8},{10,11... | collective-permute-start | bytes 1572872 | tf_op jit(solution)/shard_map/ppermute | solution.py:12
  76.5 5.9 %copy-start.8 = (f32[2,512,128]{2,1,0:T(8,128)}, f32[2,512,128]{2,1,0:T(8,128)S(1)}, u32[]{:S(2)}) copy-start(f32[2,512,128]{2,1,0:T(8,128)S(1)} %collective-permute-done) | copy-start | bytes 1572868
  76.5 13.8 %collective-permute-start.16 = (f32[2,8,64,128]{3,2,1,0:T(8,128)S(1)}, f32[2,8,64,128]{3,2,1,0:T(8,128)}, u32[]{:S(2)}, u32[]{:S(2)}) collective-permute-start(f32[2,8,64,128]{3,2,1,0:T(8,128)S(1)} %bitcast.17), channel_id=1, source_target_pairs={{0,1},{1,0},{2,3},{3,2},{4,5},{5,4},{6,7},{7,6},{8,9},{9,8},{10,11... | collective-permute-start | bytes 1572872 | tf_op jit(solution)/shard_map/ppermute | solution.py:12
  77.0 18.1 %collective-permute-start.11 = (f32[2,8,64,128]{3,2,1,0:T(8,128)S(1)}, f32[2,8,64,128]{3,2,1,0:T(8,128)}, u32[]{:S(2)}, u32[]{:S(2)}) collective-permute-start(f32[2,8,64,128]{3,2,1,0:T(8,128)S(1)} %bitcast.15), channel_id=1, source_target_pairs={{0,1},{1,0},{2,3},{3,2},{4,5},{5,4},{6,7},{7,6},{8,9},{9,8},{10,11... | collective-permute-start | bytes 1572872 | tf_op jit(solution)/shard_map/ppermute | solution.py:12
  77.1 22.9 %collective-permute-start.6 = (f32[2,8,64,128]{3,2,1,0:T(8,128)S(1)}, f32[2,8,64,128]{3,2,1,0:T(8,128)}, u32[]{:S(2)}, u32[]{:S(2)}) collective-permute-start(f32[2,8,64,128]{3,2,1,0:T(8,128)S(1)} %bitcast.13), channel_id=1, source_target_pairs={{0,1},{1,0},{2,3},{3,2},{4,5},{5,4},{6,7},{7,6},{8,9},{9,8},{10,11... | collective-permute-start | bytes 1572872 | tf_op jit(solution)/shard_map/ppermute | solution.py:12
  78.3 26.5 %collective-permute-start.1 = (f32[2,8,64,128]{3,2,1,0:T(8,128)S(1)}, f32[2,8,64,128]{3,2,1,0:T(8,128)S(1)}, u32[]{:S(2)}, u32[]{:S(2)}) collective-permute-start(f32[2,8,64,128]{3,2,1,0:T(8,128)S(1)} %bitcast.11), channel_id=1, source_target_pairs={{0,1},{1,0},{2,3},{3,2},{4,5},{5,4},{6,7},{7,6},{8,9},{9,8},{10,11... | collective-permute-start | bytes 1572872 | tf_op jit(solution)/shard_map/ppermute | solution.py:12
  82.4 27.4 %collective-permute-start.37 = (f32[2,8,64,128]{3,2,1,0:T(8,128)}, f32[2,8,64,128]{3,2,1,0:T(8,128)S(1)}, u32[]{:S(2)}, u32[]{:S(2)}) collective-permute-start(f32[2,8,64,128]{3,2,1,0:T(8,128)} %level_product.54.own), channel_id=1, source_target_pairs={{0,4},{1,5},{2,6},{3,7},{4,0},{5,1},{6,2},{7,3},{8,12},{9,13},{10,... | collective-permute-start | bytes 1572872 | tf_op jit(solution)/shard_map/ppermute | solution.py:12
  90.2 24.6 %collective-permute-start.32 = (f32[2,8,64,128]{3,2,1,0:T(8,128)}, f32[2,8,64,128]{3,2,1,0:T(8,128)S(1)}, u32[]{:S(2)}, u32[]{:S(2)}) collective-permute-start(f32[2,8,64,128]{3,2,1,0:T(8,128)} %level_product.50.own), channel_id=1, source_target_pairs={{0,2},{1,3},{2,0},{3,1},{4,6},{5,7},{6,4},{7,5},{8,10},{9,11},{10,... | collective-permute-start | bytes 1572872 | tf_op jit(solution)/shard_map/ppermute | solution.py:12
  95.1 27.7 %collective-permute-start.27 = (f32[2,8,64,128]{3,2,1,0:T(8,128)}, f32[2,8,64,128]{3,2,1,0:T(8,128)S(1)}, u32[]{:S(2)}, u32[]{:S(2)}) collective-permute-start(f32[2,8,64,128]{3,2,1,0:T(8,128)} %level_product.47.own), channel_id=1, source_target_pairs={{0,2},{1,3},{2,0},{3,1},{4,6},{5,7},{6,4},{7,5},{8,10},{9,11},{10,... | collective-permute-start | bytes 1572872 | tf_op jit(solution)/shard_map/ppermute | solution.py:12
  100.0 34.0 %collective-permute-start.22 = (f32[2,8,64,128]{3,2,1,0:T(8,128)}, f32[2,8,64,128]{3,2,1,0:T(8,128)S(1)}, u32[]{:S(2)}, u32[]{:S(2)}) collective-permute-start(f32[2,8,64,128]{3,2,1,0:T(8,128)} %level_product.44.own), channel_id=1, source_target_pairs={{0,2},{1,3},{2,0},{3,1},{4,6},{5,7},{6,4},{7,5},{8,10},{9,11},{10,... | collective-permute-start | bytes 1572872 | tf_op jit(solution)/shard_map/ppermute | solution.py:12
  104.9 40.5 %collective-permute-start.17 = (f32[2,8,64,128]{3,2,1,0:T(8,128)}, f32[2,8,64,128]{3,2,1,0:T(8,128)}, u32[]{:S(2)}, u32[]{:S(2)}) collective-permute-start(f32[2,8,64,128]{3,2,1,0:T(8,128)} %level_product.41.own), channel_id=1, source_target_pairs={{0,2},{1,3},{2,0},{3,1},{4,6},{5,7},{6,4},{7,5},{8,10},{9,11},{10,... | collective-permute-start | bytes 1572872 | tf_op jit(solution)/shard_map/ppermute | solution.py:12
  109.9 46.6 %collective-permute-start.12 = (f32[2,8,64,128]{3,2,1,0:T(8,128)}, f32[2,8,64,128]{3,2,1,0:T(8,128)S(1)}, u32[]{:S(2)}, u32[]{:S(2)}) collective-permute-start(f32[2,8,64,128]{3,2,1,0:T(8,128)} %level_product.38.own), channel_id=1, source_target_pairs={{0,2},{1,3},{2,0},{3,1},{4,6},{5,7},{6,4},{7,5},{8,10},{9,11},{10,... | collective-permute-start | bytes 1572872 | tf_op jit(solution)/shard_map/ppermute | solution.py:12
  114.9 52.9 %collective-permute-start.7 = (f32[2,8,64,128]{3,2,1,0:T(8,128)}, f32[2,8,64,128]{3,2,1,0:T(8,128)S(1)}, u32[]{:S(2)}, u32[]{:S(2)}) collective-permute-start(f32[2,8,64,128]{3,2,1,0:T(8,128)} %level_product.35.own), channel_id=1, source_target_pairs={{0,2},{1,3},{2,0},{3,1},{4,6},{5,7},{6,4},{7,5},{8,10},{9,11},{10,... | collective-permute-start | bytes 1572872 | tf_op jit(solution)/shard_map/ppermute | solution.py:12
  122.8 56.2 %collective-permute-start.2 = (f32[2,8,64,128]{3,2,1,0:T(8,128)}, f32[2,8,64,128]{3,2,1,0:T(8,128)S(1)}, u32[]{:S(2)}, u32[]{:S(2)}) collective-permute-start(f32[2,8,64,128]{3,2,1,0:T(8,128)} %level_product.32.own), channel_id=1, source_target_pairs={{0,2},{1,3},{2,0},{3,1},{4,6},{5,7},{6,4},{7,5},{8,10},{9,11},{10,... | collective-permute-start | bytes 1572872 | tf_op jit(solution)/shard_map/ppermute | solution.py:12
  134.0 50.0 %collective-permute-start.38 = (f32[2,8,64,128]{3,2,1,0:T(8,128)}, f32[2,8,64,128]{3,2,1,0:T(8,128)S(1)}, u32[]{:S(2)}, u32[]{:S(2)}) collective-permute-start(f32[2,8,64,128]{3,2,1,0:T(8,128)} %level_product.55.own), channel_id=1, source_target_pairs={{0,8},{1,9},{2,10},{3,11},{4,12},{5,13},{6,14},{7,15},{8,0},{9,1},... | collective-permute-start | bytes 1572872 | tf_op jit(solution)/shard_map/ppermute | solution.py:12
  145.4 45.0 %collective-permute-start.33 = (f32[2,8,64,128]{3,2,1,0:T(8,128)}, f32[2,8,64,128]{3,2,1,0:T(8,128)S(1)}, u32[]{:S(2)}, u32[]{:S(2)}) collective-permute-start(f32[2,8,64,128]{3,2,1,0:T(8,128)} %level_product.51.own), channel_id=1, source_target_pairs={{0,4},{1,5},{2,6},{3,7},{4,0},{5,1},{6,2},{7,3},{8,12},{9,13},{10,... | collective-permute-start | bytes 1572872 | tf_op jit(solution)/shard_map/ppermute | solution.py:12
  156.5 43.9 %collective-permute-start.28 = (f32[2,8,64,128]{3,2,1,0:T(8,128)}, f32[2,8,64,128]{3,2,1,0:T(8,128)S(1)}, u32[]{:S(2)}, u32[]{:S(2)}) collective-permute-start(f32[2,8,64,128]{3,2,1,0:T(8,128)} %level_product.48.own), channel_id=1, source_target_pairs={{0,4},{1,5},{2,6},{3,7},{4,0},{5,1},{6,2},{7,3},{8,12},{9,13},{10,... | collective-permute-start | bytes 1572872 | tf_op jit(solution)/shard_map/ppermute | solution.py:12
  167.7 43.9 %collective-permute-start.23 = (f32[2,8,64,128]{3,2,1,0:T(8,128)}, f32[2,8,64,128]{3,2,1,0:T(8,128)S(1)}, u32[]{:S(2)}, u32[]{:S(2)}) collective-permute-start(f32[2,8,64,128]{3,2,1,0:T(8,128)} %level_product.45.own), channel_id=1, source_target_pairs={{0,4},{1,5},{2,6},{3,7},{4,0},{5,1},{6,2},{7,3},{8,12},{9,13},{10,... | collective-permute-start | bytes 1572872 | tf_op jit(solution)/shard_map/ppermute | solution.py:12
  179.0 43.9 %collective-permute-start.18 = (f32[2,8,64,128]{3,2,1,0:T(8,128)}, f32[2,8,64,128]{3,2,1,0:T(8,128)S(1)}, u32[]{:S(2)}, u32[]{:S(2)}) collective-permute-start(f32[2,8,64,128]{3,2,1,0:T(8,128)} %level_product.42.own), channel_id=1, source_target_pairs={{0,4},{1,5},{2,6},{3,7},{4,0},{5,1},{6,2},{7,3},{8,12},{9,13},{10,... | collective-permute-start | bytes 1572872 | tf_op jit(solution)/shard_map/ppermute | solution.py:12
  184.0 6.3 %copy-start = (f32[2,8,64,128]{3,2,1,0:T(8,128)}, f32[2,8,64,128]{3,2,1,0:T(8,128)S(1)}, u32[]{:S(2)}) copy-start(f32[2,8,64,128]{3,2,1,0:T(8,128)S(1)} %collective-permute-done.38.other) | copy-start | bytes 1572868
  184.0 50.1 %collective-permute-start.13 = (f32[2,8,64,128]{3,2,1,0:T(8,128)}, f32[2,8,64,128]{3,2,1,0:T(8,128)S(1)}, u32[]{:S(2)}, u32[]{:S(2)}) collective-permute-start(f32[2,8,64,128]{3,2,1,0:T(8,128)} %level_product.39.own), channel_id=1, source_target_pairs={{0,4},{1,5},{2,6},{3,7},{4,0},{5,1},{6,2},{7,3},{8,12},{9,13},{10,... | collective-permute-start | bytes 1572872 | tf_op jit(solution)/shard_map/ppermute | solution.py:12
  190.3 6.3 %copy-start.23 = (f32[2,8,64,128]{3,2,1,0:T(8,128)}, f32[2,8,64,128]{3,2,1,0:T(8,128)S(1)}, u32[]{:S(2)}) copy-start(f32[2,8,64,128]{3,2,1,0:T(8,128)S(1)} %collective-permute-done.33.other) | copy-start | bytes 1572868
  190.3 55.1 %collective-permute-start.8 = (f32[2,8,64,128]{3,2,1,0:T(8,128)}, f32[2,8,64,128]{3,2,1,0:T(8,128)}, u32[]{:S(2)}, u32[]{:S(2)}) collective-permute-start(f32[2,8,64,128]{3,2,1,0:T(8,128)} %level_product.36.own), channel_id=1, source_target_pairs={{0,4},{1,5},{2,6},{3,7},{4,0},{5,1},{6,2},{7,3},{8,12},{9,13},{10,... | collective-permute-start | bytes 1572872 | tf_op jit(solution)/shard_map/ppermute | solution.py:12
  200.4 7.4 %copy-start.24 = (f32[2,8,64,128]{3,2,1,0:T(8,128)}, f32[2,8,64,128]{3,2,1,0:T(8,128)S(1)}, u32[]{:S(2)}) copy-start(f32[2,8,64,128]{3,2,1,0:T(8,128)S(1)} %collective-permute-done.28.other) | copy-start | bytes 1572868
  200.4 56.0 %collective-permute-start.3 = (f32[2,8,64,128]{3,2,1,0:T(8,128)}, f32[2,8,64,128]{3,2,1,0:T(8,128)}, u32[]{:S(2)}, u32[]{:S(2)}) collective-permute-start(f32[2,8,64,128]{3,2,1,0:T(8,128)} %level_product.33.own), channel_id=1, source_target_pairs={{0,4},{1,5},{2,6},{3,7},{4,0},{5,1},{6,2},{7,3},{8,12},{9,13},{10,... | collective-permute-start | bytes 1572872 | tf_op jit(solution)/shard_map/ppermute | solution.py:12
  211.6 49.3 %collective-permute-start.34 = (f32[2,8,64,128]{3,2,1,0:T(8,128)}, f32[2,8,64,128]{3,2,1,0:T(8,128)S(1)}, u32[]{:S(2)}, u32[]{:S(2)}) collective-permute-start(f32[2,8,64,128]{3,2,1,0:T(8,128)} %level_product.52.own), channel_id=1, source_target_pairs={{0,8},{1,9},{2,10},{3,11},{4,12},{5,13},{6,14},{7,15},{8,0},{9,1},... | collective-permute-start | bytes 1572872 | tf_op jit(solution)/shard_map/ppermute | solution.py:12
  222.9 43.4 %collective-permute-start.29 = (f32[2,8,64,128]{3,2,1,0:T(8,128)}, f32[2,8,64,128]{3,2,1,0:T(8,128)S(1)}, u32[]{:S(2)}, u32[]{:S(2)}) collective-permute-start(f32[2,8,64,128]{3,2,1,0:T(8,128)} %level_product.49.own), channel_id=1, source_target_pairs={{0,8},{1,9},{2,10},{3,11},{4,12},{5,13},{6,14},{7,15},{8,0},{9,1},... | collective-permute-start | bytes 1572872 | tf_op jit(solution)/shard_map/ppermute | solution.py:12
  234.1 44.5 %collective-permute-start.24 = (f32[2,8,64,128]{3,2,1,0:T(8,128)}, f32[2,8,64,128]{3,2,1,0:T(8,128)S(1)}, u32[]{:S(2)}, u32[]{:S(2)}) collective-permute-start(f32[2,8,64,128]{3,2,1,0:T(8,128)} %level_product.46.own), channel_id=1, source_target_pairs={{0,8},{1,9},{2,10},{3,11},{4,12},{5,13},{6,14},{7,15},{8,0},{9,1},... | collective-permute-start | bytes 1572872 | tf_op jit(solution)/shard_map/ppermute | solution.py:12
  245.4 37.8 %collective-permute-start.19 = (f32[2,8,64,128]{3,2,1,0:T(8,128)}, f32[2,8,64,128]{3,2,1,0:T(8,128)S(1)}, u32[]{:S(2)}, u32[]{:S(2)}) collective-permute-start(f32[2,8,64,128]{3,2,1,0:T(8,128)} %level_product.43.own), channel_id=1, source_target_pairs={{0,8},{1,9},{2,10},{3,11},{4,12},{5,13},{6,14},{7,15},{8,0},{9,1},... | collective-permute-start | bytes 1572872 | tf_op jit(solution)/shard_map/ppermute | solution.py:12
  256.4 31.5 %collective-permute-start.14 = (f32[2,8,64,128]{3,2,1,0:T(8,128)}, f32[2,8,64,128]{3,2,1,0:T(8,128)S(1)}, u32[]{:S(2)}, u32[]{:S(2)}) collective-permute-start(f32[2,8,64,128]{3,2,1,0:T(8,128)} %level_product.40.own), channel_id=1, source_target_pairs={{0,8},{1,9},{2,10},{3,11},{4,12},{5,13},{6,14},{7,15},{8,0},{9,1},... | collective-permute-start | bytes 1572872 | tf_op jit(solution)/shard_map/ppermute | solution.py:12
  260.9 31.7 %collective-permute-start.9 = (f32[2,8,64,128]{3,2,1,0:T(8,128)}, f32[2,8,64,128]{3,2,1,0:T(8,128)S(1)}, u32[]{:S(2)}, u32[]{:S(2)}) collective-permute-start(f32[2,8,64,128]{3,2,1,0:T(8,128)} %level_product.37.own), channel_id=1, source_target_pairs={{0,8},{1,9},{2,10},{3,11},{4,12},{5,13},{6,14},{7,15},{8,0},{9,1},... | collective-permute-start | bytes 1572872 | tf_op jit(solution)/shard_map/ppermute | solution.py:12
  266.3 31.0 %collective-permute-start.4 = (f32[2,8,64,128]{3,2,1,0:T(8,128)}, f32[2,8,64,128]{3,2,1,0:T(8,128)S(1)}, u32[]{:S(2)}, u32[]{:S(2)}) collective-permute-start(f32[2,8,64,128]{3,2,1,0:T(8,128)} %level_product.34.own), channel_id=1, source_target_pairs={{0,8},{1,9},{2,10},{3,11},{4,12},{5,13},{6,14},{7,15},{8,0},{9,1},... | collective-permute-start | bytes 1572872 | tf_op jit(solution)/shard_map/ppermute | solution.py:12
  (23 other events, 81.0 us)
